TPU v7x, 32 devices: a whole 2x2x4 slice. The times are simulated.
32 devices in a mesh: parts: 2 (over y), rows: 16 (over z, x, core).
Axes of the slice: x: 2, y: 2, z: 4, core: 2. Of those that a mesh axis runs over, the one named last changes fastest.
Arguments:
- factor_panels: float32 [16384, 1536], P(('parts', 'rows')), parts along dimension 0, as said below
- targets: float32 [16384, 256], P(('parts', 'rows')), parts along dimension 0, may hold values from -6 to 6
- later_solutions: float32 [16384, 256], P(('parts', 'rows')), parts along dimension 0, as said below
Outputs:
- solved_rows: float32 [16384, 256], P(('parts', 'rows')), parts along dimension 0
There are 2 independent parts, one for each index of `parts`. A program takes and returns all parts, laid end to end along the dimension named above; each array names one. Nothing has to cross between parts.
Inputs may be any that keep to these rules, and one draw needn't show every extreme that they name: `factor_panels`: in rows of block d < 3, column blocks above d are zero and column block d holds a lower-triangular inverse diagonal block. `later_solutions`: the first 1536 rows are zero.
All inputs are finite; a program needn't handle non-finite values.
Results may differ from a plain program's by a relative error of at most 0.0001.
Values sent between devices are 32-bit elements; how exact they have to be, the bound alone decides.
A program may use at most 64 MiB of HBM per device.

v0:
```python
import jax
import jax.numpy as jnp
from jax import lax
from jax.sharding import PartitionSpec as P

exact_mode = lax.Precision.HIGHEST


def broadcast(shard, axis, root):
    mine = lax.axis_index(axis) == root
    return lax.psum(jnp.where(mine, shard, jnp.zeros_like(shard)), axis)


def product(left, right):
    return jnp.dot(left, right, precision=exact_mode, preferred_element_type=jnp.float32)


def transposed(left, right):
    return lax.dot_general(
        left,
        right,
        (((0,), (0,)), ((), ())),
        precision=exact_mode,
        preferred_element_type=jnp.float32,
    )


def local(factor_panels, targets, later_solutions):
    device = lax.axis_index("rows")
    block_rows = factor_panels.shape[0]
    panels = factor_panels.shape[1] // block_rows

    def panel_cols(panel):
        return factor_panels[:, panel * block_rows : (panel + 1) * block_rows]

    solved = []
    residual = targets
    for panel in range(panels):
        candidate = product(panel_cols(panel), residual)
        forward_part = broadcast(candidate, "rows", panel)
        solved.append(forward_part)
        residual = jnp.where(
            device > panel, residual - product(panel_cols(panel), forward_part), residual
        )
    answer = later_solutions
    for panel in reversed(range(panels)):
        partial_terms = jnp.where(device > panel, transposed(panel_cols(panel), answer), 0.0)
        fan_sum = lax.psum(partial_terms, "rows")
        candidate = transposed(panel_cols(panel), solved[panel] - fan_sum)
        answer = jnp.where(device == panel, candidate, answer)
    return jnp.where(device < panels, answer, residual)


def solution(mesh):
    in_specs = (P(("parts", "rows"), None), P(("parts", "rows"), None), P(("parts", "rows"), None))
    out_specs = P(("parts", "rows"), None)
    return jax.shard_map(local, mesh=mesh, in_specs=in_specs, out_specs=out_specs, check_vma=False)
```

profile of v0, /device:TPU:1, one launch (start us, length us, event | category | flops | bytes accessed | tf_op | source)
XLA Modules:
  0.0 503.3 jit_solution(16484655578196028900)
XLA Ops:
  6.5 3.3 convolution_select_fusion.5
  9.9 0.0 all-reduce.9.cloned.1.call-start
  9.9 93.7 %all-reduce.7.cloned.1.call-done = f32[512,256]{1,0:T(8,128)} async-done(((f32[512,256]{1,0:T(8,128)}), f32[512,256]{1,0:T(8,128)}) %all-reduce.7.cloned.1.call-update) | async-done | bytes 524304 | tf_op jit(solution)/shard_map/psum | solution.py:11
  103.6 2.5 fusion.13
  106.2 0.8 copy-done.5
  106.9 1.8 fusion.11
  108.8 0.0 all-reduce.15.cloned.1.call-start
  108.8 3.7 convolution_select_fusion.2
  112.5 87.0 %all-reduce.9.cloned.1.call-done = f32[512,256]{1,0:T(8,128)} async-done(((f32[512,256]{1,0:T(8,128)}), f32[512,256]{1,0:T(8,128)}) %all-reduce.9.cloned.1.call-update) | async-done | bytes 524304 | tf_op jit(solution)/shard_map/psum | solution.py:11
  199.5 2.2 fusion.10
  201.7 0.8 copy-done.1
  202.5 1.8 fusion.8
  204.4 92.6 %all-reduce.15.cloned.1.call-done = (f32[512,256]{1,0:T(8,128)}, f32[512,256]{1,0:T(8,128)}) async-done(((f32[512,256]{1,0:T(8,128)}, f32[512,256]{1,0:T(8,128)}), (f32[512,256]{1,0:T(8,128)}, f32[512,256]{1,0:T(8,128)})) %all-reduce.15.cloned.1.call-update) | async-done | bytes 1048592 | tf_op jit(solution)/shard_map/psum | solution.py:11
  296.9 3.2 fusion.7
  300.1 0.8 copy-done.4
  300.9 2.6 fusion.6
  303.6 0.2 all-reduce.13.cloned.1.call-start
  303.8 90.6 %all-reduce.11.cloned.1.call-done = f32[512,256]{1,0:T(8,128)} async-done(((f32[512,256]{1,0:T(8,128)}), f32[512,256]{1,0:T(8,128)}) %all-reduce.11.cloned.1.call-update) | async-done | bytes 524304 | tf_op jit(solution)/shard_map/psum | solution.py:48
  394.4 3.0 fusion.5
  397.4 0.8 copy-done.3
  398.2 2.6 fusion.4
  400.9 90.8 %all-reduce.13.cloned.1.call-done = f32[512,256]{1,0:T(8,128)} async-done(((f32[512,256]{1,0:T(8,128)}), f32[512,256]{1,0:T(8,128)}) %all-reduce.13.cloned.1.call-update) | async-done | bytes 524304 | tf_op jit(solution)/shard_map/psum | solution.py:48
  491.7 3.3 fusion.3
  495.0 1.8 fusion.2
  (17 shorter events, 0.2 us)
Async XLA Ops:
  6.5 100.4 %copy-start = (f32[512,1536]{1,0:T(8,128)S(1)}, f32[512,1536]{1,0:T(8,128)}, u32[]{:S(2)}) copy-start(f32[512,1536]{1,0:T(8,128)} %param.3) | copy-start | bytes 9437188
  6.5 97.1 %all-reduce.7.cloned.1.call-start = ((), (), s32[]{:S(2)}) async-start(), calls=%async_computation | async-start | bytes 1048576 | tf_op jit(solution)/shard_map/psum | solution.py:11
  9.9 189.6 %all-reduce.9.cloned.1.call-start = ((), (), s32[]{:S(2)}) async-start(), calls=%async_computation.1 | async-start | bytes 1048576 | tf_op jit(solution)/shard_map/psum | solution.py:11
  106.1 0.8 copy-start.5
  108.8 188.2 %all-reduce.15.cloned.1.call-start = ((), (), s32[]{:S(2)}) async-start(), calls=%async_computation.4 | async-start | bytes 2097152 | tf_op jit(solution)/shard_map/psum | solution.py:11
  201.7 0.8 copy-start.1
  204.3 190.1 %all-reduce.11.cloned.1.call-start = ((), (), s32[]{:S(2)}) async-start(), calls=%async_computation.2 | async-start | bytes 1048576 | tf_op jit(solution)/shard_map/psum | solution.py:48
  300.1 0.8 copy-start.4
  303.6 188.1 %all-reduce.13.cloned.1.call-start = ((), (), s32[]{:S(2)}) async-start(), calls=%async_computation.3 | async-start | bytes 1048576 | tf_op jit(solution)/shard_map/psum | solution.py:48
  397.4 0.8 copy-start.3
  491.7 3.3 copy-start.2
  491.7 3.3 copy-start.6
Sparse Core Ops, SparseCore 0:
  10.8 92.7 all-reduce.6
  108.9 90.5 all-reduce.8
  204.4 92.4 all-reduce.14
  303.7 90.6 all-reduce.10
  401.0 90.6 all-reduce.12
where the time goes:
time: 504 us; the launch traced here: 503 us
  waiting for transfers between devices  455 us (90%)
  matrix products  31.8 us (6%)
  between operations  13.3 us (3%)
    psum x3, waiting for transfers between devices, broadcast(): return lax.psum(jnp.where(mine, shard, jnp.zeros_like(shard)), axis)  273 us
    psum x2, waiting for transfers between devices, local(): fan_sum = lax.psum(partial_terms, 'rows')  181 us
    dot_general x6, matrix products, transposed(): lax.dot_general(left, right, (((0,), (0,)), ((), ())), precision=exact_mo...  18.3 us
    dot_general x6, matrix products, product(): jnp.dot(left, right, precision=exact_mode, preferred_element_type=jnp.flo...  13.5 us
  transfers between devices with their start and end apart: 5, of which 5 were waited for; matrix products, arithmetic and copies ran while one was open for 1% of the time, Pallas kernels for 0%

commit v1 on v0

--- a/solution.py
+++ b/solution.py
@@ -45,7 +45,7 @@
     answer = later_solutions
     for panel in reversed(range(panels)):
         partial_terms = jnp.where(device > panel, transposed(panel_cols(panel), answer), 0.0)
-        fan_sum = lax.psum(partial_terms, "rows")
+        fan_sum = jnp.sum(lax.all_gather(partial_terms, "rows"), axis=0)
         candidate = transposed(panel_cols(panel), solved[panel] - fan_sum)
         answer = jnp.where(device == panel, candidate, answer)
     return jnp.where(device < panels, answer, residual)

time: 504 us -> 579 us (1.15); the launches traced: 503 us -> 572 us
  waiting for transfers between devices: 455 us -> 485 us
  local copies, waits for them, and re-layouts: 3.15 us -> 29.4 us
  other arithmetic: 0 us -> 11.9 us
    all_gather x0 -> x3, waiting for transfers between devices: none -> 220 us  [local(): fan_sum = jnp.sum(lax.all_gather(partial_terms, 'rows'), axis=0)]
    psum x2 -> x0, waiting for transfers between devices: 181 us -> none  [local(): fan_sum = lax.psum(partial_terms, 'rows')]
    unnamed x14 -> x20, local copies, waits for them, and re-layouts: 3.15 us -> 25.3 us
    reduce_sum x0 -> x3, other arithmetic: none -> 11.9 us  [local(): fan_sum = jnp.sum(lax.all_gather(partial_terms, 'rows'), axis=0)]
    psum x3, waiting for transfers between devices: 273 us -> 266 us  [broadcast(): return lax.psum(jnp.where(mine, shard, jnp.zeros_like(shard)), axis)]
  transfers between devices with their start and end apart: 5 -> 6, of which waited for: 5 -> 6; matrix products, arithmetic and copies ran while one was open for 1% -> 3% of each run, Pallas kernels for 0% -> 0%
where the time goes in v1:
time: 579 us; the launch traced here: 572 us
  waiting for transfers between devices  485 us (84%)
  matrix products  30.9 us (5%)
  local copies, waits for them, and re-layouts  29.4 us (5%)
  between operations  13.9 us (2%)
  other arithmetic  11.9 us (2%)
    psum x3, waiting for transfers between devices, broadcast(): return lax.psum(jnp.where(mine, shard, jnp.zeros_like(shard)), axis)  266 us
    all_gather x3, waiting for transfers between devices, local(): fan_sum = jnp.sum(lax.all_gather(partial_terms, 'rows'), axis=0)  220 us
    unnamed x20, local copies, waits for them, and re-layouts  25.3 us
    dot_general x6, matrix products, transposed(): lax.dot_general(left, right, (((0,), (0,)), ((), ())), precision=exact_mo...  15.6 us
    dot_general x6, matrix products, product(): jnp.dot(left, right, precision=exact_mode, preferred_element_type=jnp.flo...  15.2 us
    reduce_sum x3, other arithmetic, local(): fan_sum = jnp.sum(lax.all_gather(partial_terms, 'rows'), axis=0)  11.9 us
  transfers between devices with their start and end apart: 6, of which 6 were waited for; matrix products, arithmetic and copies ran while one was open for 3% of the time, Pallas kernels for 0%

profile of v1, /device:TPU:1, one launch (start us, length us, event | category | flops | bytes accessed | tf_op | source)
XLA Modules:
  0.0 572.1 jit_solution(14324012116021466383)
XLA Ops:
  6.5 3.3 convolution_select_fusion.5
  9.9 93.7 %all-reduce.4.cloned.1.call-done = f32[512,256]{1,0:T(8,128)} async-done(((f32[512,256]{1,0:T(8,128)}), f32[512,256]{1,0:T(8,128)}) %all-reduce.4.cloned.1.call-update) | async-done | bytes 524304 | tf_op jit(solution)/shard_map/psum | solution.py:11
  103.6 2.5 fusion.13
  106.9 2.7 fusion.11
  109.7 3.7 convolution_select_fusion.2
  113.5 86.9 %all-reduce.6.cloned.1.call-done = f32[512,256]{0,1:T(8,128)} async-done(((f32[512,256]{0,1:T(8,128)}), f32[512,256]{0,1:T(8,128)}) %all-reduce.6.cloned.1.call-update) | async-done | bytes 524304 | tf_op jit(solution)/shard_map/psum | solution.py:11
  200.4 2.2 fusion.10
  203.4 2.7 fusion.8
  206.6 71.2 %all-gather.7.cloned.1.call-done = f32[8192,256]{1,0:T(8,128)} async-done(((f32[512,256]{1,0:T(8,128)}), f32[8192,256]{1,0:T(8,128)}) %all-gather.7.cloned.1.call-update) | async-done | bytes 8388624 | tf_op jit(solution)/shard_map/all_gather | solution.py:48
  277.8 4.8 reduce_sum.27
  282.6 2.0 copy.12
  284.6 85.0 %all-reduce.8.cloned.1.call-done = f32[512,256]{0,1:T(8,128)} async-done(((f32[512,256]{0,1:T(8,128)}), f32[512,256]{0,1:T(8,128)}) %all-reduce.8.cloned.1.call-update) | async-done | bytes 524304 | tf_op jit(solution)/shard_map/psum | solution.py:11
  369.6 3.2 fusion.7
  373.6 1.9 fusion.6
  375.5 75.3 %all-gather.9.cloned.1.call-done = f32[8192,256]{0,1:T(8,128)} async-done(((f32[512,256]{0,1:T(8,128)}), f32[8192,256]{0,1:T(8,128)}) %all-gather.9.cloned.1.call-update) | async-done | bytes 8388624 | tf_op jit(solution)/shard_map/all_gather | solution.py:48
  450.8 10.9 %copy.24 = f32[32,8,16,512]{3,2,1,0:T(8,128)S(1)} copy(f32[32,8,16,512]{3,1,2,0:T(8,128)} %bitcast.62) | data formatting | bytes 16777216
  461.8 3.3 bitcast_reduce_fusion.1
  467.7 1.9 fusion.4
  469.6 73.3 %all-gather.11.cloned.1.call-done = f32[8192,256]{0,1:T(8,128)} async-done(((f32[512,256]{0,1:T(8,128)}), f32[8192,256]{0,1:T(8,128)}) %all-gather.11.cloned.1.call-update) | async-done | bytes 8388624 | tf_op jit(solution)/shard_map/all_gather | solution.py:48
  542.9 11.2 %copy.25 = f32[32,8,16,512]{3,2,1,0:T(8,128)S(1)} copy(f32[32,8,16,512]{3,1,2,0:T(8,128)} %bitcast.61) | data formatting | bytes 16777216
  554.1 3.8 bitcast_reduce_fusion
  557.9 2.0 copy.15
  559.9 3.3 fusion.3
  563.2 1.8 fusion.2
  (31 shorter events, 5.8 us)
Async XLA Ops:
  6.5 100.4 %copy-start = (f32[512,1536]{1,0:T(8,128)S(1)}, f32[512,1536]{1,0:T(8,128)}, u32[]{:S(2)}) copy-start(f32[512,1536]{1,0:T(8,128)} %param.3) | copy-start | bytes 9437188
  6.5 97.1 %all-reduce.4.cloned.1.call-start = ((), (), s32[]{:S(2)}) async-start(), calls=%async_computation | async-start | bytes 1048576 | tf_op jit(solution)/shard_map/psum | solution.py:11
  9.9 190.5 %all-reduce.6.cloned.1.call-start = ((), (), s32[]{:S(2)}) async-start(), calls=%async_computation.1 | async-start | bytes 1048576 | tf_op jit(solution)/shard_map/psum | solution.py:11
  106.1 0.8 copy-start.3
  109.7 168.1 %all-gather.7.cloned.1.call-start = ((), (), s32[]{:S(2)}) async-start(), calls=%async_computation.3 | async-start | bytes 8912896 | tf_op jit(solution)/shard_map/all_gather | solution.py:48
  113.4 256.2 %all-reduce.8.cloned.1.call-start = ((), (), s32[]{:S(2)}) async-start(), calls=%async_computation.2 | async-start | bytes 1048576 | tf_op jit(solution)/shard_map/psum | solution.py:11
  202.6 0.8 copy-start.1
  206.1 244.7 %all-gather.9.cloned.1.call-start = ((), (), s32[]{:S(2)}) async-start(), calls=%async_computation.4 | async-start | bytes 8912896 | tf_op jit(solution)/shard_map/all_gather | solution.py:48
  372.8 0.8 copy-start.5
  375.5 167.4 %all-gather.11.cloned.1.call-start = ((), (), s32[]{:S(2)}) async-start(), calls=%async_computation.5 | async-start | bytes 8912896 | tf_op jit(solution)/shard_map/all_gather | solution.py:48
  461.8 3.3 copy-start.6
  461.8 3.3 copy-start.8
  466.9 0.8 copy-start.4
  559.9 3.3 copy-start.2
  559.9 3.3 copy-start.7
Sparse Core Ops, SparseCore 0:
  10.8 92.7 all-reduce.3
  109.8 90.5 all-reduce.5
  202.5 75.1 all-gather.6
  281.0 88.5 all-reduce.7
  375.6 75.1 all-gather.8
  469.7 73.1 all-gather.10
